TPU v7x, 1024 devices: a whole 8x8x8 slice. The times are simulated.
1024 devices in a mesh: elem: 128 (over y, z, core), band: 8 (over x).
Axes of the slice: x: 8, y: 8, z: 8, core: 2. Of those that a mesh axis runs over, the one named last changes fastest.
Arguments:
- psi: bfloat16 [2, 128, 4096, 240], P(None, 'elem', 'band'), may hold values from -6 to 6
- h_diag: bfloat16 [128, 240, 240], P('elem'), may hold values from -0.375 to 0.375
- h_face: bfloat16 [128, 6, 240, 240], P('elem'), may hold values from -0.375 to 0.375
- adjacency: int32 [128, 6], P('elem'), may hold values from 0 to 127, as said below
- nbasis: int32 [128], P('elem'), may hold values from 60 to 240
Outputs:
- psi_next: bfloat16 [2, 128, 4096, 240], P(None, 'elem', 'band')
- intersection: float32 [512, 2, 4096], P('elem', None, 'band')
- density: float32 [128, 240], P('elem')
Inputs may be any that keep to these rules, and one draw needn't show every extreme that they name: `adjacency`: the neighbour across each face lies in the same block of 1 consecutive elements as the element, in the previous block or in the next one, counted cyclically; face 0 always in the previous block, face 1 always in the next.
All inputs are finite; a program needn't handle non-finite values.
Results may differ from a plain program's by a relative error of at most 0.0032.
Values may be sent and summed in bfloat16 or wider, within the bound.
A program may use at most 32 MiB of HBM per device.

v0:
```python
import jax
import jax.numpy as jnp
from jax import lax
from jax.sharding import PartitionSpec as P

ITERS = 2


half_step = 0.1


def with_halo(cells, sides, width):
    for axis, dim in sides:
        count = lax.axis_size(axis)
        head = lax.slice_in_dim(cells, 0, width, axis=dim)
        tail = lax.slice_in_dim(cells, cells.shape[dim] - width, cells.shape[dim], axis=dim)
        cells = jnp.concatenate(
            [
                lax.ppermute(tail, axis, [(i, (i + 1) % count) for i in range(count)]),
                cells,
                lax.ppermute(head, axis, [((i + 1) % count, i) for i in range(count)]),
            ],
            axis=dim,
        )
    return cells


def flatten_rows(block):
    return jnp.transpose(block, (0, 2, 1, 3)).reshape(
        block.shape[0], block.shape[2], block.shape[1] * block.shape[3]
    )


def group_terms(left_real, left_imag, right_real, right_imag):
    sum_real = jnp.dot(left_real, right_real.T, preferred_element_type=jnp.float32) + jnp.dot(
        left_imag, right_imag.T, preferred_element_type=jnp.float32
    )
    sum_imag = jnp.dot(left_imag, right_real.T, preferred_element_type=jnp.float32) - jnp.dot(
        left_real, right_imag.T, preferred_element_type=jnp.float32
    )
    return jnp.stack([sum_real, sum_imag], axis=1)


def apply_hamiltonian(total, h_diag, h_face, local_index, keep):
    elements = total.shape[1]
    extended = with_halo(total, (("elem", 1),), elements)
    near = jnp.take(extended, local_index.reshape(-1), axis=1)
    near = near.reshape(2, elements, local_index.shape[1], total.shape[2], total.shape[3])
    image = jnp.einsum("ceob,ekb->ceok", total, h_diag, preferred_element_type=jnp.float32)
    image = image + jnp.einsum("cefob,efkb->ceok", near, h_face, preferred_element_type=jnp.float32)
    return jnp.where(keep, image, jnp.zeros_like(image))


def shards(psi, h_diag, h_face, adjacency, nbasis):
    elements = psi.shape[1]
    own_orbitals = psi.shape[2]
    basis_width = psi.shape[3]
    groups_elem = lax.axis_size("elem")
    groups_band = lax.axis_size("band")
    mask = jnp.arange(basis_width, dtype=jnp.int32)[None, :] < nbasis[:, None]
    keep = mask[None, :, None, :]
    psi0 = jnp.where(keep, psi, jnp.zeros_like(psi))
    first_global = (lax.axis_index("elem") - 1) * elements
    local_index = jnp.mod(adjacency - first_global, elements * groups_elem)
    base = psi0.astype(jnp.float32)
    state = psi0
    for sweep_index in range(ITERS):
        total = (base + state.astype(jnp.float32)).astype(jnp.bfloat16)
        image = apply_hamiltonian(total, h_diag, h_face, local_index, keep)
        real_part = base[0] + half_step * image[1]
        imag_part = base[1] - half_step * image[0]
        state = jnp.stack([real_part, imag_part]).astype(jnp.bfloat16)
    squares_sum = jnp.sum(jnp.square(state.astype(jnp.float32)), axis=(0, 2))
    density = lax.psum(squares_sum * (1.0 / (own_orbitals * groups_band)), "band")
    scale = 1.0 / (elements * groups_elem * basis_width)
    own_rows = flatten_rows(state)
    whole_terms = group_terms(own_rows[0], own_rows[1], own_rows[0], own_rows[1]) * scale
    intersection = lax.psum_scatter(whole_terms, "elem", scatter_dimension=0, tiled=True)
    return (state, intersection, density)


def solution(mesh):
    return jax.shard_map(
        shards,
        mesh=mesh,
        in_specs=(
            P(None, "elem", "band", None),
            P("elem", None, None),
            P("elem", None, None, None),
            P("elem", None),
            P("elem"),
        ),
        out_specs=(P(None, "elem", "band", None), P("elem", None, "band"), P("elem", None)),
        check_vma=False,
    )
```

profile of v0, /device:TPU:1, one launch (start us, length us, event | category | flops | bytes accessed | tf_op | source)
XLA Modules:
  0.0 288.8 jit_solution(8072050029781845976)
XLA Ops:
  7.2 0.0 copy-start
  7.2 0.0 copy-start.4
  7.2 0.0 all-reduce.3.cloned.1.call-start
  8.0 1.2 add_convert_fusion.1
  9.2 0.0 copy-start.1
  9.2 6.3 %collective-permute-start = (bf16[2,1,512,240]{2,3,0,1:T(8,128)(2,1)S(1)}, bf16[2,1,512,240]{2,3,0,1:T(8,128)(2,1)S(1)}, u32[]{:S(2)}, u32[]{:S(2)}) collective-permute-start(bf16[2,1,512,240]{2,3,0,1:T(8,128)(2,1)S(1)} %add_convert_fusion.1), channel_id=1, source_target_pairs={{0,8},{8,16},{16,24},{24,32},{32,40},{40,48},{48,56},{56,64},{64,7... | collective-permute-start | bytes 1474568 | tf_op jit(solution)/shard_map/ppermute | solution.py:19
  15.5 11.7 %collective-permute-start.1 = (bf16[2,1,512,240]{2,3,0,1:T(8,128)(2,1)S(1)}, bf16[2,1,512,240]{2,3,0,1:T(8,128)(2,1)}, u32[]{:S(2)}, u32[]{:S(2)}) collective-permute-start(bf16[2,1,512,240]{2,3,0,1:T(8,128)(2,1)S(1)} %add_convert_fusion.1), channel_id=1, source_target_pairs={{8,0},{16,8},{24,16},{32,24},{40,32},{48,40},{56,48},{64,56},{72,6... | collective-permute-start | bytes 1474568 | tf_op jit(solution)/shard_map/ppermute | solution.py:21
  27.2 0.7 compare_and_fusion
  27.9 1.2 fusion.56
  29.1 0.0 copy-done.4
  29.1 1.2 fusion.54
  30.3 0.0 collective-permute-done
  30.3 0.0 copy-done.1
  30.3 0.0 copy-start.3
  30.3 0.8 copy-done.3
  31.1 0.0 collective-permute-done.1
  31.1 1.5 pad_maximum_fusion
  32.6 2.4 gather_fusion
  35.0 0.0 copy-done
  35.0 3.1 %fusion.33 = f32[2,1,512,240]{2,3,0,1:T(8,128)S(1)} fusion(f32[2,512,240]{1,2,0:T(8,128)} %fusion.54, bf16[6,2,512,240]{2,3,1,0:T(8,128)(2,1)} %gather_fusion, pred[6]{0:T(512)(128)(4,1)S(1)} %get-tuple-element.10, bf16[1,6,240,240]{3,2,1,0:T(8,128)(2,1)S(1)} %copy-done, pred[240]{0:T(512)(128)(4,1)S(1)} %iota_compare_fusion), kind=kOutput, calls=%fused_computation.26 | convolution fusion | flops 709754880 | bytes 5606646 | tf_op jit(solution)/shard_map/cefob,efkb->ceok/dot_general | solution.py:50
  38.2 0.0 copy-start.2
  38.2 0.2 fusion.51
  38.4 0.8 copy-done.2
  39.2 0.2 add_convert_fusion
  39.4 1.9 collective-permute-start.2
  41.3 10.2 %collective-permute-start.3 = (bf16[2,1,512,240]{2,3,0,1:T(8,128)(2,1)S(1)}, bf16[2,1,512,240]{2,3,0,1:T(8,128)(2,1)S(1)}, u32[]{:S(2)}, u32[]{:S(2)}) collective-permute-start(bf16[2,1,512,240]{2,3,0,1:T(8,128)(2,1)S(1)} %add_convert_fusion), channel_id=1, source_target_pairs={{8,0},{16,8},{24,16},{32,24},{40,32},{48,40},{56,48},{64,56},{72,6... | collective-permute-start | bytes 1474568 | tf_op jit(solution)/shard_map/ppermute | solution.py:21
  51.6 1.2 fusion.52
  52.8 0.0 collective-permute-done.2
  52.8 0.2 collective-permute-done.3
  53.1 0.2 pad_maximum_fusion.1
  53.2 2.4 gather_fusion.1
  55.7 3.1 %fusion.39 = f32[2,1,512,240]{2,3,0,1:T(8,128)S(1)} fusion(f32[2,512,240]{1,2,0:T(8,128)} %fusion.52, bf16[6,2,512,240]{2,3,1,0:T(8,128)(2,1)} %gather_fusion.1, pred[6]{0:T(512)(128)(4,1)S(1)} %get-tuple-element.10, bf16[1,6,240,240]{3,2,1,0:T(8,128)(2,1)S(1)} %copy-done, pred[240]{0:T(512)(128)(4,1)S(1)} %iota_compare_fusion), kind=kOutput, calls=%fused_computation.28 | convolution fusion | flops 709754880 | bytes 5606646 | tf_op jit(solution)/shard_map/cefob,efkb->ceok/dot_general | solution.py:50
  58.8 0.2 fusion.47
  59.0 0.3 fusion.64
  59.4 0.3 fusion.59
  59.7 0.3 fusion.11
  60.0 0.3 fusion.10
  60.4 1.6 maximum_multiply_fusion
  62.0 0.0 all-reduce.3.cloned.1.call-update
  62.0 1.3 dynamic-slice
  63.9 0.2 multiply_reduce_fusion
  64.1 13.8 %psum.7 = f32[1,240]{1,0:T(1,128)} all-reduce(f32[1,240]{1,0:T(1,128)S(1)} %bitcast.123), channel_id=1, replica_groups=mesh['elem'=128,'band'=8] {'band'}, use_global_device_ids=true, to_apply=%region_2.4 | all-reduce | flops 240 | bytes 1920 | tf_op jit(solution)/shard_map/psum | solution.py:74
  77.9 0.8 fusion.57
  78.7 201.9 %all-reduce.3.cloned.1.call-done = f32[512,2,512]{2,0,1:T(8,128)} async-done(((f32[512,2,512]{2,0,1:T(8,128)}), f32[512,2,512]{2,0,1:T(8,128)}) %all-reduce.3.cloned.1.call-update) | async-done | bytes 2097168
  280.6 0.8 constant_dynamic-slice_fusion
  281.4 0.6 copy.17
  (3 shorter events, 0.0 us)
Async XLA Ops:
  7.2 27.9 %copy-start = (bf16[1,6,240,240]{3,2,1,0:T(8,128)(2,1)S(1)}, bf16[1,6,240,240]{3,2,1,0:T(8,128)(2,1)}, u32[]{:S(2)}) copy-start(bf16[1,6,240,240]{3,2,1,0:T(8,128)(2,1)} %param.9) | copy-start | bytes 2073604
  7.2 21.9 %copy-start.4 = (bf16[1,240,240]{2,1,0:T(8,128)(2,1)S(1)}, bf16[1,240,240]{2,1,0:T(8,128)(2,1)}, u32[]{:S(2)}) copy-start(bf16[1,240,240]{2,1,0:T(8,128)(2,1)} %param.8) | copy-start | bytes 345604
  7.2 273.4 %all-reduce.3.cloned.1.call-start = ((), (), s32[]{:S(2)}) async-start(), calls=%async_computation | async-start | bytes 4194304
  9.2 21.1 %copy-start.1 = (bf16[2,1,512,240]{2,3,0,1:T(8,128)(2,1)}, bf16[2,1,512,240]{2,3,0,1:T(8,128)(2,1)S(1)}, u32[]{:S(2)}) copy-start(bf16[2,1,512,240]{2,3,0,1:T(8,128)(2,1)S(1)} %add_convert_fusion.1) | copy-start | bytes 1474564
  9.2 21.1 %collective-permute-start = (bf16[2,1,512,240]{2,3,0,1:T(8,128)(2,1)S(1)}, bf16[2,1,512,240]{2,3,0,1:T(8,128)(2,1)S(1)}, u32[]{:S(2)}, u32[]{:S(2)}) collective-permute-start(bf16[2,1,512,240]{2,3,0,1:T(8,128)(2,1)S(1)} %add_convert_fusion.1), channel_id=1, source_target_pairs={{0,8},{8,16},{16,24},{24,32},{32,40},{40,48},{48,56},{56,64},{64,7... | collective-permute-start | bytes 1474568 | tf_op jit(solution)/shard_map/ppermute | solution.py:19
  15.5 15.6 %collective-permute-start.1 = (bf16[2,1,512,240]{2,3,0,1:T(8,128)(2,1)S(1)}, bf16[2,1,512,240]{2,3,0,1:T(8,128)(2,1)}, u32[]{:S(2)}, u32[]{:S(2)}) collective-permute-start(bf16[2,1,512,240]{2,3,0,1:T(8,128)(2,1)S(1)} %add_convert_fusion.1), channel_id=1, source_target_pairs={{8,0},{16,8},{24,16},{32,24},{40,32},{48,40},{56,48},{64,56},{72,6... | collective-permute-start | bytes 1474568 | tf_op jit(solution)/shard_map/ppermute | solution.py:21
  30.3 0.8 copy-start.3
  38.2 1.0 copy-start.2
  39.4 13.4 %collective-permute-start.2 = (bf16[2,1,512,240]{2,3,0,1:T(8,128)(2,1)S(1)}, bf16[2,1,512,240]{2,3,0,1:T(8,128)(2,1)S(1)}, u32[]{:S(2)}, u32[]{:S(2)}) collective-permute-start(bf16[2,1,512,240]{2,3,0,1:T(8,128)(2,1)S(1)} %add_convert_fusion), channel_id=1, source_target_pairs={{0,8},{8,16},{16,24},{24,32},{32,40},{40,48},{48,56},{56,64},{64,7... | collective-permute-start | bytes 1474568 | tf_op jit(solution)/shard_map/ppermute | solution.py:19
  41.3 11.7 %collective-permute-start.3 = (bf16[2,1,512,240]{2,3,0,1:T(8,128)(2,1)S(1)}, bf16[2,1,512,240]{2,3,0,1:T(8,128)(2,1)S(1)}, u32[]{:S(2)}, u32[]{:S(2)}) collective-permute-start(bf16[2,1,512,240]{2,3,0,1:T(8,128)(2,1)S(1)} %add_convert_fusion), channel_id=1, source_target_pairs={{8,0},{16,8},{24,16},{32,24},{40,32},{48,40},{56,48},{64,56},{72,6... | collective-permute-start | bytes 1474568 | tf_op jit(solution)/shard_map/ppermute | solution.py:21
Sparse Core Ops, SparseCore 0:
  62.1 218.4 all-reduce.2
where the time goes:
time: 291 us; the launch traced here: 289 us
  waiting for transfers between devices  202 us (69%)
  starting transfers between devices  30.2 us (10%)
  between operations  15.6 us (5%)
  blocking collectives  13.8 us (5%)
  matrix products  10 us (3%)
  local copies, waits for them, and re-layouts  9.08 us (3%)
  other arithmetic  8 us (3%)
    unnamed x2, waiting for transfers between devices  202 us
    ppermute x2, starting transfers between devices, with_halo(): lax.ppermute(head, axis, [((i + 1) % count, i) for i in range(count)])  21.9 us
    psum x1, blocking collectives, shards(): lax.psum(squares_sum * (1.0 / (own_orbitals * groups_band)), 'band')  13.8 us
    ppermute x2, starting transfers between devices, with_halo(): lax.ppermute(tail, axis, [(i, (i + 1) % count) for i in range(count)])  8.22 us
    dot_general x2, matrix products, apply_hamiltonian(): jnp.einsum('cefob,efkb->ceok', near, h_face, preferred_element_type=jnp.f...  6.27 us
  transfers between devices with their start and end apart: 5, of which 2 were waited for; matrix products, arithmetic and copies ran while one was open for 2% of the time, Pallas kernels for 0%

commit v1 on v0

v1 whole, which is shorter than its diff:
```python
import functools

import jax
import jax.numpy as jnp
from jax import lax
from jax.experimental import pallas as pl
from jax.experimental.pallas import tpu as pltpu
from jax.sharding import PartitionSpec as P

MESH = pl.DeviceIdType.MESH
F32 = jnp.float32
BF16 = jnp.bfloat16
HALF_STEP = 0.1


def dot(a, b):
    return jnp.dot(a, b, preferred_element_type=F32)


def dot_nt(a, b):
    return lax.dot_general(a, b, (((1,), (1,)), ((), ())), preferred_element_type=F32)


def kernel(
    side, bands, chunks, adj, nb, psi, hd, hf, out_psi, out_int, out_den,
    psi_v, hd_v, hf_v, hm, t0, t0f, t0n, t1, t1f, t1n, xo, xp, pick, sel, own, gs, gr, s2, s2r, dac, dens, denr,
    load_sem, out_sem, h_send, h_recv, p_send, p_recv, g_send, g_recv, r_send, r_recv, d_send, d_recv,
):
    elems = side * side * 2
    faces = hf.shape[0]
    basis = hd.shape[0]
    group = xo.shape[2]
    width = group // chunks
    peers = side - 1
    turn = [side // 2 + (k // 2 if k % 2 == 0 else -(k + 1) // 2) for k in range(side)]

    e = lax.axis_index("elem")
    band = lax.axis_index("band")
    core = e % 2
    chip = e // 2
    y, z = chip // side, chip % side
    far = (e + elems - 1 + 2 * core) % elems
    near = e + 1 - 2 * core

    def along(first, r):
        by_y = core if not first else 1 - core
        yy = (y + by_y * r) % side
        zz = (z + (1 - by_y) * r) % side
        return (yy * side + zz) * 2 + core

    firsts = [along(True, r) for r in turn[:-1]]
    seconds = [along(False, r) for r in turn[:-1]]
    others = [(band + r) % bands for r in range(1, bands)]

    loads = []
    for i in range(chunks):
        for c in range(2):
            copy = pltpu.make_async_copy(
                psi.at[c, :, pl.ds(i * width, width)], psi_v.at[i, :, pl.ds(c * width, width)], load_sem.at[2 * i + c]
            )
            copy.start()
            loads.append(copy)
    load_hd = pltpu.make_async_copy(hd, hd_v, load_sem.at[2 * chunks])
    load_hf = pltpu.make_async_copy(hf, hf_v, load_sem.at[2 * chunks + 1])
    load_hd.start()
    load_hf.start()

    barrier = pltpu.get_barrier_semaphore()
    everyone = [(far, band), (near, band)]
    everyone += [(d, band) for d in firsts + seconds]
    everyone += [(e, b) for b in others]
    for d in everyone:
        pl.semaphore_signal(barrier, inc=1, device_id=d, device_id_type=MESH)

    block = group // 2 // side
    t = lax.broadcasted_iota(jnp.int32, (group // 2, group), 0)
    o = lax.broadcasted_iota(jnp.int32, (group // 2, group), 1)
    k = t // block
    r = side // 2 + jnp.where(k % 2 == 0, k // 2, 0 - (k + 1) // 2)
    position = (1 - core) * y + core * z
    d = (position + r) % side
    j = t % block
    q = j // 4
    orbital = ((1 - core) * (d * side + q) + core * (q * side + d)) * 8 + core * 4 + j % 4
    pick[...] = jnp.where(orbital == o, 1.0, 0.0).astype(BF16)

    keep = lax.broadcasted_iota(jnp.int32, (basis, 2 * width), 0) < nb[0]

    pl.semaphore_wait(barrier, len(everyone))

    def halo(sweep, i, src, dst, to_far):
        s = (sweep * 2 + to_far) * chunks + i
        return pltpu.make_async_remote_copy(
            src_ref=src.at[i], dst_ref=dst.at[i], send_sem=h_send.at[s], recv_sem=h_recv.at[s],
            device_id=(far if to_far else near, band), device_id_type=MESH,
        )

    sent = []
    for i in range(chunks):
        loads[2 * i].wait()
        loads[2 * i + 1].wait()
        t0[i] = jnp.where(keep, psi_v[i].astype(F32), 0.0).astype(BF16)
        for copy in (halo(0, i, t0, t0f, 1), halo(0, i, t0, t0n, 0)):
            copy.start()
            sent.append(copy)

    load_hd.wait()
    load_hf.wait()
    weights = [[jnp.where(adj[0, f] == s, 1.0, 0.0).astype(F32) for f in range(faces)] for s in (e, far, near)]
    strip = 16

    def prepare(n, carry):
        rows = pl.ds(pl.multiple_of(n * strip, strip), strip)
        low = pl.ds(pl.multiple_of(basis + n * strip, strip), strip)
        valid = lax.broadcasted_iota(jnp.int32, (strip, basis), 0) + n * strip < nb[0]
        faces_f32 = [hf_v[f, rows, :].astype(F32) for f in range(faces)]
        for s in range(3):
            total = hd_v[rows, :].astype(F32) if s == 0 else jnp.zeros((strip, basis), F32)
            for f in range(faces):
                total = total + weights[s][f] * faces_f32[f]
            total = jnp.where(valid, total, 0.0)
            high = total.astype(BF16)
            hm[s, rows, :] = high
            hm[s, low, :] = (total - high.astype(F32)).astype(BF16)
        return carry

    lax.fori_loop(0, basis // strip, prepare, 0)

    def image(i, mine, other, beside):
        both = dot(hm[0], mine[i]) + dot(hm[1], other[i]) + dot(hm[2], beside[i])
        return both[:basis] + both[basis:]

    for i in range(chunks):
        halo(0, i, t0, t0n, 0).wait_recv()
        halo(0, i, t0, t0f, 1).wait_recv()
        im = image(i, t0, t0f, t0n)
        base = t0[i].astype(F32)
        turned = jnp.concatenate([im[:, width:], -im[:, :width]], axis=1)
        state = (base + (2 * HALF_STEP) * turned).astype(BF16)
        t1[i] = (base + state.astype(F32)).astype(BF16)
        for copy in (halo(1, i, t1, t1f, 1), halo(1, i, t1, t1n, 0)):
            copy.start()
            sent.append(copy)

    def to_partner(i):
        lanes = pl.ds(i * width, width)
        return pltpu.make_async_remote_copy(
            src_ref=xo.at[:, :, lanes], dst_ref=xp.at[:, :, lanes], send_sem=p_send.at[i], recv_sem=p_recv.at[i],
            device_id=(near, band), device_id_type=MESH,
        )

    stores = []
    dac[...] = jnp.zeros_like(dac)
    for i in range(chunks):
        halo(1, i, t1, t1n, 0).wait_recv()
        halo(1, i, t1, t1f, 1).wait_recv()
        im = image(i, t1, t1f, t1n)
        base = t0[i].astype(F32)
        lanes = pl.ds(i * width, width)
        real = (base[:, :width] + HALF_STEP * im[:, width:]).astype(BF16)
        imag = (base[:, width:] - HALF_STEP * im[:, :width]).astype(BF16)
        xo[0, :, lanes] = real
        xo[1, :, lanes] = imag
        copy = to_partner(i)
        copy.start()
        sent.append(copy)
        copy = pltpu.make_async_copy(xo.at[:, :, lanes], out_psi.at[:, :, lanes], out_sem.at[i])
        copy.start()
        stores.append(copy)
        real, imag = real.astype(F32), imag.astype(F32)
        dac[:basis, :] += real * real + imag * imag

    column = jnp.transpose(dac[...])
    part = column[0:8]
    for n in range(1, width // 8):
        part = part + column[8 * n : 8 * n + 8]
    dens[...] = part
    for n in range(bands - 1):
        copy = pltpu.make_async_remote_copy(
            src_ref=dens, dst_ref=denr.at[n], send_sem=d_send.at[n], recv_sem=d_recv.at[n],
            device_id=(e, others[n]), device_id_type=MESH,
        )
        copy.start()
        sent.append(copy)

    for c in range(2):
        sel[c] = dot_nt(pick[...], xo[c]).astype(BF16)
    for i in range(chunks):
        to_partner(i).wait_recv()
    for c in range(2):
        sel[2 + c] = dot_nt(pick[...], xp[c]).astype(BF16)

    def first(k):
        return pltpu.make_async_remote_copy(
            src_ref=gs.at[k], dst_ref=gr.at[k], send_sem=g_send.at[k], recv_sem=g_recv.at[k],
            device_id=(firsts[k], band), device_id_type=MESH,
        )

    per = max(side // 2, 1)
    for h in range(side // per):
        rows = pl.ds(h * per * block, per * block)
        total = None
        for source, at in ((xo, 0), (xp, 2)):
            left, right = sel[at, rows, :], sel[at + 1, rows, :]
            term = dot(jnp.concatenate([left, right], axis=0), source[0])
            term = term + dot(jnp.concatenate([right, -left], axis=0), source[1])
            total = term if total is None else total + term
        for b in range(per):
            k = h * per + b
            a = slice(b * block, (b + 1) * block)
            c = slice((per + b) * block, (per + b + 1) * block)
            if k < peers:
                gs[k, :block, :] = total[a].astype(BF16)
                gs[k, block:, :] = total[c].astype(BF16)
                copy = first(k)
                copy.start()
                sent.append(copy)
            else:
                own[:block, :] = total[a]
                own[block:, :] = total[c]

    for k in range(peers):
        first(k).wait_recv()
    upper = lax.broadcasted_iota(jnp.int32, (8, group), 0) < 4
    for m in range(block // 8):
        tiles = []
        for at in (8 * m, block + 8 * m):
            tile = own[at : at + 8, :]
            for k in range(peers):
                tile = tile + gr[k, at : at + 8, :].astype(F32)
            tiles.append(tile)
        s2[2 * m] = jnp.where(upper, tiles[0], pltpu.roll(tiles[1], 4, 0))
        s2[2 * m + 1] = jnp.where(upper, pltpu.roll(tiles[0], 4, 0), tiles[1])

    place = core * y + (1 - core) * z

    def second(k):
        return pltpu.make_async_remote_copy(
            src_ref=s2.at[(place + turn[k]) % side], dst_ref=s2r.at[k], send_sem=r_send.at[k], recv_sem=r_recv.at[k],
            device_id=(seconds[k], band), device_id_type=MESH,
        )

    for k in range(peers):
        copy = second(k)
        copy.start()
        sent.append(copy)
    part = dens[...]
    for n in range(bands - 1):
        pltpu.make_async_remote_copy(
            src_ref=dens, dst_ref=denr.at[n], send_sem=d_send.at[n], recv_sem=d_recv.at[n],
            device_id=(e, others[n]), device_id_type=MESH,
        ).wait_recv()
        part = part + denr[n]
    whole = jnp.sum(part, axis=0, keepdims=True) * (1.0 / (group * bands))
    out_den[...] = whole[:, :basis]
    result = s2[place]
    for k in range(peers):
        second(k).wait_recv()
        result = result + s2r[k]
    result = result * (1.0 / (elems * basis))
    for n in range(4):
        out_int[n, 0:1, :] = result[n : n + 1]
        out_int[n, 1:2, :] = result[4 + n : 5 + n]

    for copy in stores:
        copy.wait()
    for copy in sent:
        copy.wait_send()


def shards(side, bands, chunks, psi, h_diag, h_face, adjacency, nbasis):
    group, basis = psi.shape[2], psi.shape[3]
    faces = h_face.shape[1]
    width = group // chunks
    half = group // 2
    block = half // side
    peers = side - 1
    dma = pltpu.SemaphoreType.DMA
    anywhere = pl.BlockSpec(memory_space=pl.ANY)
    hbm = pl.BlockSpec(memory_space=pltpu.HBM)
    scalars = pl.BlockSpec(memory_space=pltpu.SMEM)
    vmem = pl.BlockSpec(memory_space=pltpu.VMEM)
    chunked = pltpu.VMEM((chunks, basis, 2 * width), BF16)
    out_psi, out_int, out_den = pl.pallas_call(
        functools.partial(kernel, side, bands, chunks),
        out_shape=(
            jax.ShapeDtypeStruct((2, basis, group), BF16),
            jax.ShapeDtypeStruct((4, 2, group), F32),
            jax.ShapeDtypeStruct((1, basis), F32),
        ),
        in_specs=[scalars, scalars, hbm, hbm, hbm],
        out_specs=(anywhere, vmem, vmem),
        scratch_shapes=[
            chunked,
            pltpu.VMEM((basis, basis), BF16),
            pltpu.VMEM((faces, basis, basis), BF16),
            pltpu.VMEM((3, 2 * basis, basis), BF16),
            *[chunked] * 6,
            pltpu.VMEM((2, basis, group), BF16),
            pltpu.VMEM((2, basis, group), BF16),
            pltpu.VMEM((half, group), BF16),
            pltpu.VMEM((4, half, basis), BF16),
            pltpu.VMEM((2 * block, group), F32),
            pltpu.VMEM((peers, 2 * block, group), BF16),
            pltpu.VMEM((peers, 2 * block, group), BF16),
            pltpu.VMEM((side, 8, group), F32),
            pltpu.VMEM((peers, 8, group), F32),
            pltpu.VMEM((256, width), F32),
            pltpu.VMEM((8, 256), F32),
            pltpu.VMEM((bands - 1, 8, 256), F32),
            dma((2 * chunks + 2,)),
            dma((chunks,)),
            dma((4 * chunks,)),
            dma((4 * chunks,)),
            dma((chunks,)),
            dma((chunks,)),
            dma((peers,)),
            dma((peers,)),
            dma((peers,)),
            dma((peers,)),
            dma((bands - 1,)),
            dma((bands - 1,)),
        ],
        compiler_params=pltpu.CompilerParams(
            collective_id=0, has_side_effects=True, vmem_limit_bytes=62 * 10**6
        ),
        name="step",
    )(
        adjacency,
        nbasis,
        jnp.transpose(psi, (1, 0, 3, 2))[0],
        h_diag[0],
        h_face[0],
    )
    return jnp.transpose(out_psi, (0, 2, 1))[:, None], out_int, out_den


def build(mesh, side, chunks):
    bands = mesh.shape["band"]
    return jax.shard_map(
        functools.partial(shards, side, bands, chunks),
        mesh=mesh,
        in_specs=(
            P(None, "elem", "band", None),
            P("elem", None, None),
            P("elem", None, None, None),
            P("elem", None),
            P("elem"),
        ),
        out_specs=(P(None, "elem", "band", None), P("elem", None, "band"), P("elem", None)),
        check_vma=False,
    )


def solution(mesh):
    return build(mesh, 8, 4)
```

time: 291 us -> 57.5 us (0.20)
  waiting for transfers between devices: 202 us -> 0 us
  Pallas kernels: 0 us -> 52.9 us
  starting transfers between devices: 30.2 us -> 0 us
  between operations: 15.6 us -> 1.3 us
  blocking collectives: 13.8 us -> 0 us
  matrix products: 10 us -> 0 us
  other arithmetic: 8 us -> 0 us
  local copies, waits for them, and re-layouts: 9.08 us -> 3.08 us
    unnamed x2 -> x0, waiting for transfers between devices: 202 us -> none
    pallas_call x0 -> x1, Pallas kernels: none -> 52.9 us  [shards(): pl.pallas_call(functools.partial(kernel, side, bands, chunks), out_shape=...]
    ppermute x4 -> x0, starting transfers between devices: 30.1 us -> none  [the longest x2 21.9 us: with_halo(): lax.ppermute(head, axis, [((i + 1) % count, i) for i in range(count)])]
    psum x1 -> x0, blocking collectives: 13.8 us -> none  [shards(): lax.psum(squares_sum * (1.0 / (own_orbitals * groups_band)), 'band')]
    dot_general x8 -> x0, matrix products: 10 us -> none  [the longest x2 6.27 us: apply_hamiltonian(): jnp.einsum('cefob,efkb->ceok', near, h_face, preferred_element_type=jnp.f...]
    gather x2 -> x0, local copies, waits for them, and re-layouts: 4.86 us -> none  [apply_hamiltonian(): near = jnp.take(extended, local_index.reshape(-1), axis=1)]
  transfers between devices with their start and end apart: 5 -> 0, of which waited for: 2 -> 0; matrix products, arithmetic and copies ran while one was open for 2% -> 0% of each run, Pallas kernels for 0% -> 0%
where the time goes in v1:
time: 57.5 us; the launch traced here: 57.3 us
  Pallas kernels  52.9 us (92%)
  local copies, waits for them, and re-layouts  3.08 us (5%)
  between operations  1.3 us (2%)
    pallas_call x1, Pallas kernels, shards(): pl.pallas_call(functools.partial(kernel, side, bands, chunks), out_shape=...  52.9 us
    unnamed x7, local copies, waits for them, and re-layouts  3.08 us

profile of v1, /device:TPU:1, one launch (start us, length us, event | category | flops | bytes accessed | tf_op | source)
XLA Modules:
  0.0 57.3 jit_solution(12166539097596503529)
XLA Ops:
  1.3 52.9 %step.1 = (bf16[2,240,512]{2,1,0:T(8,128)(2,1)}, f32[4,2,512]{2,1,0:T(2,128)}, f32[1,240]{1,0:T(1,128)}) custom-call(s32[1,6]{1,0:T(1,128)} %adj.1, s32[1]{0:T(128)S(6)} %copy.13.nb, bf16[2,240,512]{2,1,0:T(8,128)(2,1)} %bitcast.13, bf16[240,240]{1,0:T(8,128)(2,1)} %bitcast.15, bf16[6,240,240]{2,1,0:T(8,128)(2,1)} %bitcast.12), custom_call_target="tpu_custom_call" | custom-call | tf_op jit(solution)/shard_map/step/pallas_call | solution.py:284
  54.2 0.0 copy-start
  54.2 1.8 %copy.14 = bf16[2,1,512,240]{2,3,1,0:T(8,128)(2,1)} copy(bf16[2,1,512,240]{2,3,1,0:T(8,128)(2,1)} %bitcast.14) | data formatting | bytes 983040
  56.0 0.0 copy-done
  56.0 0.0 copy-start.1
  56.0 0.6 %copy.15 = f32[4,2,512]{2,1,0:T(2,128)} copy(f32[4,2,512]{2,1,0:T(2,128)S(1)} %copy-done) | data formatting | bytes 32768
  56.6 0.1 copy-done.1
  56.7 0.6 copy.16
Async XLA Ops:
  54.2 1.9 %copy-start = (f32[4,2,512]{2,1,0:T(2,128)S(1)}, f32[4,2,512]{2,1,0:T(2,128)}, u32[]{:S(2)}) copy-start(f32[4,2,512]{2,1,0:T(2,128)} %get-tuple-element.16) | copy-start | bytes 49156
  56.0 0.7 %copy-start.1 = (f32[1,240]{1,0:T(1,128)S(1)}, f32[1,240]{1,0:T(1,128)}, u32[]{:S(2)}) copy-start(f32[1,240]{1,0:T(1,128)} %get-tuple-element.17) | copy-start | bytes 2884

commit v2 on v1

v2 whole, which is shorter than its diff:
```python
import functools

import jax
import jax.numpy as jnp
from jax import lax
from jax.experimental import pallas as pl
from jax.experimental.pallas import tpu as pltpu
from jax.sharding import PartitionSpec as P

MESH = pl.DeviceIdType.MESH
F32 = jnp.float32
BF16 = jnp.bfloat16
HALF_STEP = 0.1


def dot(a, b):
    return jnp.dot(a, b, preferred_element_type=F32)


def dot_nt(a, b):
    return lax.dot_general(a, b, (((1,), (1,)), ((), ())), preferred_element_type=F32)


def kernel(
    side, bands, chunks, pieces, adj_h, nb_h, psi, hd, hf, out_psi, out_int, out_den,
    adj, nb, psi_v, hd_v, hf_v, hm, t0, t0f, t0n, t1, t1f, t1n, xo, xp, pick, sel, own, gs, gr, s2, s2r, dac, dens,
    load_sem, few_sem, out_sem, h_send, h_recv, p_send, p_recv, g_send, g_recv, r_send, r_recv, d_send, d_recv,
):
    elems = side * side * 2
    faces = hf.shape[0]
    basis = hd.shape[0]
    group = xo.shape[2]
    width = group // chunks
    peers = side - 1
    turn = [side // 2 + (k // 2 if k % 2 == 0 else -(k + 1) // 2) for k in range(side)]

    e = lax.axis_index("elem")
    band = lax.axis_index("band")
    core = e % 2
    chip = e // 2
    y, z = chip // side, chip % side
    far = (e + elems - 1 + 2 * core) % elems
    near = e + 1 - 2 * core

    def along(first, r):
        by_y = core if not first else 1 - core
        yy = (y + by_y * r) % side
        zz = (z + (1 - by_y) * r) % side
        return (yy * side + zz) * 2 + core

    firsts = [along(True, r) for r in turn[:-1]]
    seconds = [along(False, r) for r in range(1, side)]
    reach = [r for r in (1, 2, -1, -2) if abs(r) < bands]
    if bands <= 3:
        reach = [1, -1][: bands - 1]

    barrier = pltpu.get_barrier_semaphore()
    everyone = [(far, band), (near, band)]
    everyone += [(d, band) for d in firsts + seconds]
    everyone += [(e, (band + r) % bands) for r in reach]
    for d in everyone:
        pl.semaphore_signal(barrier, inc=1, device_id=d, device_id_type=MESH)

    load_adj = pltpu.make_async_copy(adj_h, adj, few_sem.at[1])
    load_adj.start()
    loads = []
    for i in range(chunks):
        for c in range(2):
            copy = pltpu.make_async_copy(
                psi.at[c, :, pl.ds(i * width, width)], psi_v.at[i, :, pl.ds(c * width, width)], load_sem.at[2 * i + c]
            )
            copy.start()
            loads.append(copy)
    load_hd = pltpu.make_async_copy(hd, hd_v, load_sem.at[2 * chunks])
    load_hf = pltpu.make_async_copy(hf, hf_v, load_sem.at[2 * chunks + 1])
    load_hd.start()
    load_hf.start()

    keep = lax.broadcasted_iota(jnp.int32, (basis, 2 * width), 0) < nb_h[0]

    def halo(sweep, i, src, dst, to_far):
        s = (sweep * 2 + to_far) * chunks + i
        return pltpu.make_async_remote_copy(
            src_ref=src.at[i], dst_ref=dst.at[i], send_sem=h_send.at[s], recv_sem=h_recv.at[s],
            device_id=(far if to_far else near, band), device_id_type=MESH,
        )

    sent = []
    for i in range(chunks):
        loads[2 * i].wait()
        loads[2 * i + 1].wait()
        t0[i] = jnp.where(keep, psi_v[i].astype(F32), 0.0).astype(BF16)
        if i == 0:
            pl.semaphore_wait(barrier, len(everyone))
        for copy in (halo(0, i, t0, t0f, 1), halo(0, i, t0, t0n, 0)):
            copy.start()
            sent.append(copy)

    load_hd.wait()
    load_hf.wait()
    load_adj.wait()
    weights = [[jnp.where(adj[0, f] == s, 1.0, 0.0).astype(F32) for f in range(faces)] for s in (e, far, near)]
    strip = 16

    def prepare(n, carry):
        rows = pl.ds(pl.multiple_of(n * strip, strip), strip)
        low = pl.ds(pl.multiple_of(basis + n * strip, strip), strip)
        valid = lax.broadcasted_iota(jnp.int32, (strip, basis), 0) + n * strip < nb_h[0]
        faces_f32 = [hf_v[f, rows, :].astype(F32) for f in range(faces)]
        for s in range(3):
            total = hd_v[rows, :].astype(F32) if s == 0 else jnp.zeros((strip, basis), F32)
            for f in range(faces):
                total = total + weights[s][f] * faces_f32[f]
            total = jnp.where(valid, total, 0.0)
            high = total.astype(BF16)
            hm[s, rows, :] = high
            hm[s, low, :] = (total - high.astype(F32)).astype(BF16)
        return carry

    lax.fori_loop(0, basis // strip, prepare, 0)

    def image(sweep, i, mine, other, beside):
        halo(sweep, i, mine, beside, 0).wait_recv()
        both = dot(hm[0], mine[i]) + dot(hm[2], beside[i])
        halo(sweep, i, mine, other, 1).wait_recv()
        both = both + dot(hm[1], other[i])
        return both[:basis] + both[basis:]

    for i in range(chunks):
        im = image(0, i, t0, t0f, t0n)
        base = t0[i].astype(F32)
        turned = jnp.concatenate([im[:, width:], -im[:, :width]], axis=1)
        state = (base + (2 * HALF_STEP) * turned).astype(BF16)
        t1[i] = (base + state.astype(F32)).astype(BF16)
        for copy in (halo(1, i, t1, t1f, 1), halo(1, i, t1, t1n, 0)):
            copy.start()
            sent.append(copy)

    block = group // 2 // side
    part = block // pieces
    slab = min(group, 128)
    t = lax.broadcasted_iota(jnp.int32, (group // 2, slab), 0)
    o = lax.broadcasted_iota(jnp.int32, (group // 2, slab), 1)

    def split(v, size):
        return v >> (size.bit_length() - 1), v & (size - 1)

    k, j = split(t, part)
    h, k = split(k, side)
    up, odd = split(k, 2)
    r = side // 2 + jnp.where(odd == 0, up, -1 - up)
    d = ((1 - core) * y + core * z + r) & (side - 1)
    q, four = split(h * part + j, 4)
    orbital = ((1 - core) * (d * side + q) + core * (q * side + d)) * 8 + core * 4 + four
    for n in range(group // slab):
        pick[:, n * slab : (n + 1) * slab] = jnp.where(orbital == o + n * slab, 1.0, 0.0).astype(BF16)

    def to_partner(i):
        lanes = pl.ds(i * width, width)
        return pltpu.make_async_remote_copy(
            src_ref=xo.at[:, :, lanes], dst_ref=xp.at[:, :, lanes], send_sem=p_send.at[i], recv_sem=p_recv.at[i],
            device_id=(near, band), device_id_type=MESH,
        )

    stores = []
    dac[...] = jnp.zeros_like(dac)
    for i in range(chunks):
        im = image(1, i, t1, t1f, t1n)
        base = t0[i].astype(F32)
        lanes = pl.ds(i * width, width)
        real = (base[:, :width] + HALF_STEP * im[:, width:]).astype(BF16)
        imag = (base[:, width:] - HALF_STEP * im[:, :width]).astype(BF16)
        xo[0, :, lanes] = real
        xo[1, :, lanes] = imag
        copy = to_partner(i)
        copy.start()
        sent.append(copy)
        copy = pltpu.make_async_copy(xo.at[:, :, lanes], out_psi.at[:, :, lanes], out_sem.at[i])
        copy.start()
        stores.append(copy)
        real, imag = real.astype(F32), imag.astype(F32)
        dac[:basis, :] += real * real + imag * imag

    column = jnp.transpose(dac[...])
    some = column[0:8]
    for n in range(1, width // 8):
        some = some + column[8 * n : 8 * n + 8]
    dens[band] = some

    def density(n, to, slot):
        slot = (band + slot) % bands
        return pltpu.make_async_remote_copy(
            src_ref=dens.at[slot], dst_ref=dens.at[slot], send_sem=d_send.at[n], recv_sem=d_recv.at[n],
            device_id=(e, (band + to) % bands), device_id_type=MESH,
        )

    for n, r in enumerate(reach):
        copy = density(n, r, 0)
        copy.start()
        sent.append(copy)
    passed = [(2, -2), (2, -1), (-2, 1)] if bands == 8 else []

    for c in range(2):
        sel[c] = dot_nt(pick[...], xo[c]).astype(BF16)
    for i in range(chunks):
        to_partner(i).wait_recv()
    for c in range(2):
        sel[2 + c] = dot_nt(pick[...], xp[c]).astype(BF16)

    def first(h, k):
        s = h * peers + k
        return pltpu.make_async_remote_copy(
            src_ref=gs.at[s], dst_ref=gr.at[s], send_sem=g_send.at[s], recv_sem=g_recv.at[s],
            device_id=(firsts[k], band), device_id_type=MESH,
        )

    high = side * part
    for h in range(pieces):
        rows = pl.ds(h * high, high)
        total = None
        for source, at in ((xo, 0), (xp, 2)):
            left, right = sel[at, rows, :], sel[at + 1, rows, :]
            term = dot(jnp.concatenate([left, right], axis=0), source[0])
            term = term + dot(jnp.concatenate([right, -left], axis=0), source[1])
            total = term if total is None else total + term
        for k in range(side):
            both = jnp.concatenate(
                [total[k * part : (k + 1) * part], total[high + k * part : high + (k + 1) * part]], axis=0
            )
            if k < peers:
                gs[h * peers + k] = both.astype(BF16)
                copy = first(h, k)
                copy.start()
                sent.append(copy)
            else:
                own[h] = both

    place = core * y + (1 - core) * z
    upper = lax.broadcasted_iota(jnp.int32, (8, group), 0) < 4

    def second(q, r):
        return pltpu.make_async_remote_copy(
            src_ref=s2.at[q], dst_ref=s2r.at[r - 1], send_sem=r_send.at[r - 1], recv_sem=r_recv.at[r - 1],
            device_id=(along(False, r), band), device_id_type=MESH,
        )

    for h in range(pieces):
        for k in range(peers):
            first(h, k).wait_recv()
        for m in range(part // 8):
            tiles = []
            for at in (8 * m, part + 8 * m):
                tile = own[h, at : at + 8, :]
                for k in range(peers):
                    tile = tile + gr[h * peers + k, at : at + 8, :].astype(F32)
                tiles.append(tile)
            q = h * (part // 4) + 2 * m
            for to, tile in (
                (q, jnp.where(upper, tiles[0], pltpu.roll(tiles[1], 4, 0))),
                (q + 1, jnp.where(upper, pltpu.roll(tiles[0], 4, 0), tiles[1])),
            ):
                s2[to] = jnp.concatenate([tile[:, : group // 2], tile[:, group // 2 :]], axis=0).astype(BF16)
            for to in (q, q + 1):
                r = (to + side - place) % side

                @pl.when(r != 0)
                def _(to=to, r=r):
                    second(to, r).start()

        if h == 0:
            for n, r in enumerate(reach):
                density(n, r, -r).wait_recv()
            for n, (to, slot) in enumerate(passed):
                copy = density(len(reach) + n, to, slot)
                copy.start()
                sent.append(copy)

    result = s2[place].astype(F32)
    for r in range(1, side):
        second((place + r) % side, r).wait_recv()
        result = result + s2r[r - 1].astype(F32)
    result = jnp.concatenate([result[:8], result[8:]], axis=1) * (1.0 / (elems * basis))
    for n in range(4):
        out_int[n, 0:1, :] = result[n : n + 1]
        out_int[n, 1:2, :] = result[4 + n : 5 + n]
    for n, (to, slot) in enumerate(passed):
        density(len(reach) + n, to, slot - to).wait_recv()
    some = dens[0]
    for n in range(1, bands):
        some = some + dens[n]
    whole = jnp.sum(some, axis=0, keepdims=True) * (1.0 / (group * bands))
    out_den[...] = whole[:, :basis]

    for r in range(1, side):
        second((place + r) % side, r).wait_send()
    for copy in stores:
        copy.wait()
    for copy in sent:
        copy.wait_send()


def finish(*refs):
    copies = [pltpu.make_async_copy(refs[n], refs[3 + n], refs[6].at[n]) for n in range(3)]
    for copy in copies:
        copy.start()
    for copy in copies:
        copy.wait()


def shards(side, bands, chunks, pieces, psi, h_diag, h_face, adjacency, nbasis):
    group, basis = psi.shape[2], psi.shape[3]
    faces = h_face.shape[1]
    width = group // chunks
    half = group // 2
    block = half // side
    peers = side - 1
    dma = pltpu.SemaphoreType.DMA
    anywhere = pl.BlockSpec(memory_space=pl.ANY)
    hbm = pl.BlockSpec(memory_space=pltpu.HBM)
    vmem = pl.BlockSpec(memory_space=pltpu.VMEM)
    chunked = pltpu.VMEM((chunks, basis, 2 * width), BF16)
    arguments = [adjacency, nbasis, jnp.transpose(psi, (1, 0, 3, 2))[0], h_diag[0], h_face[0]]
    out_shape = (
        jax.ShapeDtypeStruct((2, basis, group), BF16),
        jax.ShapeDtypeStruct((4, 2, group), F32),
        jax.ShapeDtypeStruct((1, basis), F32),
    )
    outs = pl.pallas_call(
        functools.partial(kernel, side, bands, chunks, pieces),
        out_shape=out_shape,
        in_specs=[hbm, pl.BlockSpec(memory_space=pltpu.SMEM)] + [hbm] * 3,
        out_specs=(anywhere, vmem, vmem),
        scratch_shapes=[
            pltpu.SMEM((1, faces), jnp.int32),
            pltpu.SMEM((1,), jnp.int32),
            chunked,
            pltpu.VMEM((basis, basis), BF16),
            pltpu.VMEM((faces, basis, basis), BF16),
            pltpu.VMEM((3, 2 * basis, basis), BF16),
            *[chunked] * 6,
            pltpu.VMEM((2, basis, group), BF16),
            pltpu.VMEM((2, basis, group), BF16),
            pltpu.VMEM((half, group), BF16),
            pltpu.VMEM((4, half, basis), BF16),
            pltpu.VMEM((pieces, 2 * block // pieces, group), F32),
            pltpu.VMEM((pieces * peers, 2 * block // pieces, group), BF16),
            pltpu.VMEM((pieces * peers, 2 * block // pieces, group), BF16),
            pltpu.VMEM((side, 16, half), BF16),
            pltpu.VMEM((peers, 16, half), BF16),
            pltpu.VMEM((256, width), F32),
            pltpu.VMEM((bands, 8, 256), F32),
            dma((2 * chunks + 2,)),
            dma((2,)),
            dma((chunks,)),
            dma((4 * chunks,)),
            dma((4 * chunks,)),
            dma((chunks,)),
            dma((chunks,)),
            dma((pieces * peers,)),
            dma((pieces * peers,)),
            dma((peers,)),
            dma((peers,)),
            dma((max(bands - 1, 1),)),
            dma((max(bands - 1, 1),)),
        ],
        compiler_params=pltpu.CompilerParams(
            collective_id=0, has_side_effects=True, vmem_limit_bytes=40 * 2**20
        ),
        name="step",
    )(pltpu.with_memory_space_constraint(adjacency, pltpu.HBM), nbasis, *[pltpu.with_memory_space_constraint(a, pltpu.HBM) for a in arguments[2:]])
    out_psi, out_int, out_den = pl.pallas_call(
        finish,
        out_shape=out_shape,
        in_specs=[anywhere] * 3,
        out_specs=(anywhere,) * 3,
        scratch_shapes=[dma((3,))],
        compiler_params=pltpu.CompilerParams(vmem_limit_bytes=40 * 2**20),
        name="finish",
    )(*outs)
    return jnp.transpose(out_psi, (0, 2, 1))[:, None], out_int, out_den


def build(mesh, side, chunks, pieces):
    bands = mesh.shape["band"]
    return jax.shard_map(
        functools.partial(shards, side, bands, chunks, pieces),
        mesh=mesh,
        in_specs=(
            P(None, "elem", "band", None),
            P("elem", None, None),
            P("elem", None, None, None),
            P("elem", None),
            P("elem"),
        ),
        out_specs=(P(None, "elem", "band", None), P("elem", None, "band"), P("elem", None)),
        check_vma=False,
    )


def solution(mesh):
    return build(mesh, 8, 4, 2)
```

time: 57.5 us -> 50 us (0.87)
  Pallas kernels: 52.9 us -> 48.5 us
  local copies, waits for them, and re-layouts: 3.08 us -> 0 us
    pallas_call x1 -> x2, Pallas kernels: 52.9 us -> 48.5 us  [the longest x1 47.7 us: shards(): pl.pallas_call(functools.partial(kernel, side, bands, chunks, pieces), ou...]
    unnamed x7 -> x0, local copies, waits for them, and re-layouts: 3.08 us -> none
where the time goes in v2:
time: 50 us; the launch traced here: 49.8 us
  Pallas kernels  48.5 us (97%)
  between operations  1.29 us (3%)
    pallas_call x1, Pallas kernels, shards(): pl.pallas_call(functools.partial(kernel, side, bands, chunks, pieces), ou...  47.7 us

profile of v2, /device:TPU:1, one launch (start us, length us, event | category | flops | bytes accessed | tf_op | source)
XLA Modules:
  0.0 49.8 jit_solution(4786937421094541199)
XLA Ops:
  1.3 47.7 %step.1 = (bf16[2,240,512]{2,1,0:T(8,128)(2,1)S(1)}, f32[4,2,512]{2,1,0:T(2,128)S(1)}, f32[1,240]{1,0:T(1,128)S(1)}) custom-call(s32[1,6]{1,0:T(1,128)} %adj_h.1, s32[1]{0:T(128)S(6)} %copy.10.nb_h, bf16[2,240,512]{2,1,0:T(8,128)(2,1)} %bitcast.13, bf16[240,240]{1,0:T(8,128)(2,1)} %bitcast.14, bf16[6,240,240]{2,1,0:T(8,128)(2,1)} %bitcast.12), custom_call_target="tpu_custom_call" | custom-call | tf_op jit(solution)/shard_map/step/pallas_call | solution.py:328
  49.0 0.8 %finish.1 = (bf16[2,240,512]{2,1,0:T(8,128)(2,1)}, f32[4,2,512]{2,1,0:T(2,128)}, f32[1,240]{1,0:T(1,128)}) custom-call(bf16[2,240,512]{2,1,0:T(8,128)(2,1)S(1)} %get-tuple-element.9.refs_0_, f32[4,2,512]{2,1,0:T(2,128)S(1)} %get-tuple-element.10.refs_1_, f32[1,240]{1,0:T(1,128)S(1)} %get-tuple-element.11.refs_2_), custom_call_target="tpu_custom_call" | custom-call | tf_op jit(solution)/shard_map/finish/pallas_call | solution.py:371

commit v3 on v2

--- a/solution.py
+++ b/solution.py
@@ -29,7 +29,7 @@
     elems = side * side * 2
     faces = hf.shape[0]
     basis = hd.shape[0]
-    group = xo.shape[2]
+    group = out_psi.shape[2]
     width = group // chunks
     peers = side - 1
     turn = [side // 2 + (k // 2 if k % 2 == 0 else -(k + 1) // 2) for k in range(side)]
@@ -155,10 +155,12 @@
     for n in range(group // slab):
         pick[:, n * slab : (n + 1) * slab] = jnp.where(orbital == o + n * slab, 1.0, 0.0).astype(BF16)
 
+    def joined(source, c):
+        return jnp.concatenate([source[i, c] for i in range(chunks)], axis=1)
+
     def to_partner(i):
-        lanes = pl.ds(i * width, width)
         return pltpu.make_async_remote_copy(
-            src_ref=xo.at[:, :, lanes], dst_ref=xp.at[:, :, lanes], send_sem=p_send.at[i], recv_sem=p_recv.at[i],
+            src_ref=xo.at[i], dst_ref=xp.at[i], send_sem=p_send.at[i], recv_sem=p_recv.at[i],
             device_id=(near, band), device_id_type=MESH,
         )
 
@@ -170,17 +172,19 @@
         lanes = pl.ds(i * width, width)
         real = (base[:, :width] + HALF_STEP * im[:, width:]).astype(BF16)
         imag = (base[:, width:] - HALF_STEP * im[:, :width]).astype(BF16)
-        xo[0, :, lanes] = real
-        xo[1, :, lanes] = imag
+        xo[i, 0] = real
+        xo[i, 1] = imag
         copy = to_partner(i)
         copy.start()
         sent.append(copy)
-        copy = pltpu.make_async_copy(xo.at[:, :, lanes], out_psi.at[:, :, lanes], out_sem.at[i])
+        copy = pltpu.make_async_copy(xo.at[i], out_psi.at[:, :, lanes], out_sem.at[i])
         copy.start()
         stores.append(copy)
         real, imag = real.astype(F32), imag.astype(F32)
         dac[:basis, :] += real * real + imag * imag
 
+    for c in range(2):
+        sel[c] = dot_nt(pick[...], joined(xo, c)).astype(BF16)
     column = jnp.transpose(dac[...])
     some = column[0:8]
     for n in range(1, width // 8):
@@ -200,12 +204,10 @@
         sent.append(copy)
     passed = [(2, -2), (2, -1), (-2, 1)] if bands == 8 else []
 
-    for c in range(2):
-        sel[c] = dot_nt(pick[...], xo[c]).astype(BF16)
     for i in range(chunks):
         to_partner(i).wait_recv()
     for c in range(2):
-        sel[2 + c] = dot_nt(pick[...], xp[c]).astype(BF16)
+        sel[2 + c] = dot_nt(pick[...], joined(xp, c)).astype(BF16)
 
     def first(h, k):
         s = h * peers + k
@@ -220,8 +222,8 @@
         total = None
         for source, at in ((xo, 0), (xp, 2)):
             left, right = sel[at, rows, :], sel[at + 1, rows, :]
-            term = dot(jnp.concatenate([left, right], axis=0), source[0])
-            term = term + dot(jnp.concatenate([right, -left], axis=0), source[1])
+            term = dot(jnp.concatenate([left, right], axis=0), joined(source, 0))
+            term = term + dot(jnp.concatenate([right, -left], axis=0), joined(source, 1))
             total = term if total is None else total + term
         for k in range(side):
             both = jnp.concatenate(
@@ -300,7 +302,11 @@
 
 
 def finish(*refs):
-    copies = [pltpu.make_async_copy(refs[n], refs[3 + n], refs[6].at[n]) for n in range(3)]
+    copies = [pltpu.make_async_copy(refs[n], refs[3 + n], refs[6].at[n]) for n in (1, 2)]
+    rows = refs[0].shape[1] // 3
+    for n in range(6):
+        part = (n // 3, pl.ds(n % 3 * rows, rows))
+        copies.append(pltpu.make_async_copy(refs[0].at[part], refs[3].at[part], refs[6].at[3 + n]))
     for copy in copies:
         copy.start()
     for copy in copies:
@@ -338,8 +344,8 @@
             pltpu.VMEM((faces, basis, basis), BF16),
             pltpu.VMEM((3, 2 * basis, basis), BF16),
             *[chunked] * 6,
-            pltpu.VMEM((2, basis, group), BF16),
-            pltpu.VMEM((2, basis, group), BF16),
+            pltpu.VMEM((chunks, 2, basis, width), BF16),
+            pltpu.VMEM((chunks, 2, basis, width), BF16),
             pltpu.VMEM((half, group), BF16),
             pltpu.VMEM((4, half, basis), BF16),
             pltpu.VMEM((pieces, 2 * block // pieces, group), F32),
@@ -373,7 +379,7 @@
         out_shape=out_shape,
         in_specs=[anywhere] * 3,
         out_specs=(anywhere,) * 3,
-        scratch_shapes=[dma((3,))],
+        scratch_shapes=[dma((9,))],
         compiler_params=pltpu.CompilerParams(vmem_limit_bytes=40 * 2**20),
         name="finish",
     )(*outs)

time: 50 us -> 49.9 us (level)
  no operation moved by 1% of the time
where the time goes in v3:
time: 49.9 us; the launch traced here: 49.7 us
  Pallas kernels  48.4 us (97%)
  between operations  1.29 us (3%)
    pallas_call x1, Pallas kernels, shards(): pl.pallas_call(functools.partial(kernel, side, bands, chunks, pieces), ou...  47.5 us

profile of v3, /device:TPU:1, one launch (start us, length us, event | category | flops | bytes accessed | tf_op | source)
XLA Modules:
  0.0 49.7 jit_solution(8355650945119544398)
XLA Ops:
  1.3 47.5 %step.1 = (bf16[2,240,512]{2,1,0:T(8,128)(2,1)S(1)}, f32[4,2,512]{2,1,0:T(2,128)S(1)}, f32[1,240]{1,0:T(1,128)S(1)}) custom-call(s32[1,6]{1,0:T(1,128)} %adj_h.1, s32[1]{0:T(128)S(6)} %copy.10.nb_h, bf16[2,240,512]{2,1,0:T(8,128)(2,1)} %bitcast.13, bf16[240,240]{1,0:T(8,128)(2,1)} %bitcast.14, bf16[6,240,240]{2,1,0:T(8,128)(2,1)} %bitcast.12), custom_call_target="tpu_custom_call" | custom-call | tf_op jit(solution)/shard_map/step/pallas_call | solution.py:334
  48.8 0.9 %finish.1 = (bf16[2,240,512]{2,1,0:T(8,128)(2,1)}, f32[4,2,512]{2,1,0:T(2,128)}, f32[1,240]{1,0:T(1,128)}) custom-call(bf16[2,240,512]{2,1,0:T(8,128)(2,1)S(1)} %get-tuple-element.9.refs_0_, f32[4,2,512]{2,1,0:T(2,128)S(1)} %get-tuple-element.10.refs_1_, f32[1,240]{1,0:T(1,128)S(1)} %get-tuple-element.11.refs_2_), custom_call_target="tpu_custom_call" | custom-call | tf_op jit(solution)/shard_map/finish/pallas_call | solution.py:377
